TPU v7x, 32 devices: a whole 2x2x4 slice. The times are simulated.
32 devices in a mesh: seq: 8 (over z, x), tp: 4 (over y, core).
Axes of the slice: x: 2, y: 2, z: 4, core: 2. Of those that a mesh axis runs over, the one named last changes fastest.
Arguments:
- hidden: bfloat16 [4096, 4608], P('seq', 'tp'), may hold values from -60 to 60, as said below
- norm_gain: float32 [4608], replicated, may hold values from 0.1 to 1.9
- w_query: bfloat16 [4608, 2048], P(None, 'tp'), may hold values from -0.25 to 0.25
- w_key: bfloat16 [4608, 1024], P(None, 'tp'), may hold values from -0.09375 to 0.09375
- w_value: bfloat16 [4608, 1024], P(None, 'tp'), may hold values from -0.09375 to 0.09375
- segment_ids: int32 [4096], P('seq'), may hold values from 0 to 1, as said below
- page_table: int32 [8, 4], P('seq'), may hold values from 0 to 3, each once within a row
Outputs:
- attended: bfloat16 [4096, 2048], P('seq', 'tp')
- kv_cache: bfloat16 [32, 128, 2, 1024], P(('seq', 'tp'))
Inputs may be any that keep to these rules, and one draw needn't show every extreme that they name: hidden is finite. `segment_ids`: never falling along the stream and rising by one at each document start; every number from 0 to 1 appears; no document is longer than 4096 tokens. `page_table`: each row holds every number from 0 to 3 once.
All inputs are finite; a program needn't handle non-finite values.
Results may differ from a plain program's by a relative error of at most 0.012.
The roundings to bfloat16 on the way count: a program that leaves them out, or rounds other values in their place, can miss the bound.
Values may be sent and summed in bfloat16 or wider, within the bound.
A program may use at most 128 MiB of HBM per device.

v0:
```python
import jax
import jax.numpy as jnp
from jax import lax
from jax.sharding import PartitionSpec as P

HD = 128
WIN = 4096
PAGE = 128


logit_cap = 50.0
query_scale = 144.0 ** (-0.5)
norm_eps = 1e-06
far_before = -(2**30)


def entering(value, axis, join, neutral):
    count, mine = (lax.axis_size(axis), lax.axis_index(axis))
    pieces = jax.tree.map(lambda part: lax.all_gather(part, axis), value)
    running = jax.tree.map(
        lambda part, zero: jnp.full_like(part, 0) + jnp.asarray(zero, part.dtype), value, neutral
    )

    def hop(position, running):
        longer = join(running, jax.tree.map(lambda part: part[position], pieces))
        return jax.tree.map(lambda new, old: jnp.where(position < mine, new, old), longer, running)

    return lax.fori_loop(0, count - 1, hop, running)


def shifted(block, axis, distance):
    devices = range(lax.axis_size(axis))
    route = [(i - distance, i) for i in devices if i - distance in devices]
    return lax.ppermute(block, axis, route)


def rotate(heads, positions):
    half_dim = HD // 2
    freqs = 10000.0 ** (-(jnp.arange(half_dim, dtype=jnp.float32) * (2.0 / HD)))
    angles = positions.astype(jnp.float32)[:, None] * freqs[None, :]
    cosine = jnp.cos(angles)[:, None, :]
    sine_part = jnp.sin(angles)[:, None, :]
    first_half = heads[..., :half_dim]
    second_half = heads[..., half_dim:]
    return jnp.concatenate(
        [
            first_half * cosine - second_half * sine_part,
            second_half * cosine + first_half * sine_part,
        ],
        axis=-1,
    )


def join_spans(earlier, later):
    empty_early = earlier[2] < 0
    empty_late = later[2] < 0
    crossing = jnp.where(later[3 - 1] != earlier[3], later[1], far_before)
    joined_start = jnp.maximum(jnp.maximum(earlier[0], later[0]), crossing)
    joined = (joined_start, earlier[1], earlier[2], later[3])
    return tuple(
        (
            jnp.where(empty_early, late_part, jnp.where(empty_late, early_part, join_part))
            for early_part, late_part, join_part in zip(earlier, later, joined)
        )
    )


def attend_block(carry, queries, key_vals, key_first, query_index, starts):
    numerator, totals = carry
    count = key_vals.shape[0]
    kv_heads = queries.shape[1]
    keys = key_vals[:, 0].reshape(count, kv_heads, HD)
    values = key_vals[:, 1].reshape(count, kv_heads, HD)
    scores = (
        jnp.einsum("qgrd,kgd->grqk", queries, keys, preferred_element_type=jnp.float32)
        * query_scale
    )
    capped = logit_cap * jnp.tanh(scores / logit_cap)
    key_index = key_first + jnp.arange(count, dtype=jnp.int32)
    allowed = (
        (key_index[None, :] >= starts[:, None])
        & (key_index[None, :] <= query_index[:, None])
        & (query_index[:, None] - key_index[None, :] < WIN)
    )
    weights = jnp.where(allowed, jnp.exp(capped), 0.0)
    totals = totals + jnp.sum(weights, axis=-1)
    numerator = numerator + jnp.einsum(
        "grqk,kgd->grqd", weights.astype(jnp.bfloat16), values, preferred_element_type=jnp.float32
    )
    return (numerator, totals)


def per_device(hidden, norm_gain, w_query, w_key, w_value, segment_ids, page_table):
    tokens = hidden.shape[0]
    full_rows = lax.all_gather(hidden, "tp", axis=1, tiled=True)
    wide = full_rows.astype(jnp.float32)
    meansq = jnp.mean(wide * wide, axis=-1, keepdims=True)
    normed = (wide * lax.rsqrt(meansq + norm_eps) * norm_gain).astype(jnp.bfloat16)
    queries_raw = jnp.dot(normed, w_query, preferred_element_type=jnp.float32)
    keys_raw = jnp.dot(normed, w_key, preferred_element_type=jnp.float32)
    values = jnp.dot(normed, w_value, preferred_element_type=jnp.float32).astype(jnp.bfloat16)
    place = lax.axis_index("seq")
    first_token = place * tokens
    local_index = jnp.arange(tokens, dtype=jnp.int32)
    earlier_ids = jnp.concatenate([segment_ids[:1], segment_ids[:-1]])
    inner = jnp.where(
        (local_index > 0) & (segment_ids != earlier_ids), first_token + local_index, 0
    )
    own_span = (
        jnp.max(inner).reshape(1),
        first_token.reshape(1),
        segment_ids[:1],
        segment_ids[-1:],
    )
    identity = (
        jnp.full((1,), far_before, jnp.int32),
        jnp.zeros((1,), jnp.int32),
        jnp.full((1,), -1, jnp.int32),
        jnp.full((1,), -1, jnp.int32),
    )
    prior_start, prior_first, prior_first_id, prior_last_id = entering(
        own_span, "seq", join_spans, identity
    )
    opening = jnp.where(
        (place == 0) | (prior_last_id[0] != segment_ids[0]), first_token, prior_start[0]
    )
    marks = jnp.where(local_index == 0, opening, inner)
    starts = lax.cummax(marks, axis=0)
    query_index = first_token + local_index
    positions = query_index - starts
    q_heads = w_query.shape[1] // HD
    kv_heads = w_key.shape[1] // HD
    repeat = q_heads // kv_heads
    queries = rotate(queries_raw.reshape(tokens, q_heads, HD), positions).astype(jnp.bfloat16)
    queries = queries.reshape(tokens, kv_heads, repeat, HD)
    keys = rotate(keys_raw.reshape(tokens, kv_heads, HD), positions).astype(jnp.bfloat16)
    own_block = jnp.stack([keys.reshape(tokens, kv_heads * HD), values], axis=1)
    carry = (
        jnp.zeros((kv_heads, repeat, tokens, HD), jnp.float32),
        jnp.zeros((kv_heads, repeat, tokens), jnp.float32),
    )
    carry = attend_block(carry, queries, own_block, first_token, query_index, starts)
    blocks_back = WIN // tokens

    def visit(sums, block, distance):
        key_first = first_token - distance * tokens
        return attend_block(sums, queries, block, key_first, query_index, starts)

    def advance(distance, state):
        sums, block = state
        block = shifted(block, "seq", 1)
        return (visit(sums, block, distance), block)

    carry, unused = lax.fori_loop(1, blocks_back + 1, advance, (carry, own_block))
    numerator, totals = carry
    mixed = numerator / totals[..., None]
    attended = jnp.transpose(mixed, (2, 0, 1, 3)).reshape(tokens, q_heads * HD).astype(jnp.bfloat16)
    pages_here = tokens // PAGE
    pages = own_block.reshape(pages_here, PAGE, 2, kv_heads * HD)
    table = page_table[0]
    slot_ids = jnp.arange(pages_here, dtype=jnp.int32)
    source = jnp.sum(jnp.where(table[None, :] == slot_ids[:, None], slot_ids[None, :], 0), axis=1)
    ordered = jnp.take(pages, source, axis=0)
    kv_cache = lax.all_to_all(ordered, "tp", split_axis=0, concat_axis=3, tiled=True)
    return (attended, kv_cache)


def solution(mesh):
    placed = (
        P("seq", "tp"),
        P(),
        P(None, "tp"),
        P(None, "tp"),
        P(None, "tp"),
        P("seq"),
        P("seq", None),
    )
    return jax.shard_map(
        per_device,
        mesh=mesh,
        in_specs=placed,
        out_specs=(P("seq", "tp"), P(("seq", "tp"), None, None, None)),
        check_vma=False,
    )
```

profile of v0, /device:TPU:8, one launch (start us, length us, event | category | flops | bytes accessed | tf_op | source)
XLA Modules:
  0.0 295.5 jit_solution(13842468532972447373)
XLA Ops:
  10.0 2.2 slice_dynamic-update-slice_fusion
  12.2 2.2 fusion.33
  17.3 10.5 %all-reduce.4 = (s32[8]{0:T(128)S(1)}, s32[8]{0:T(128)S(1)}, s32[8]{0:T(128)S(1)}, s32[8]{0:T(128)S(1)}) all-reduce(s32[8]{0:T(128)S(1)} %dynamic-update-slice, s32[8]{0:T(128)S(1)} %slice_dynamic-update-slice_fusion.1, s32[8]{0:T(128)S(1)} %dynamic-update-slice.2, s32[8]{0:T(128)S(1)} %get-tuple-element.494), channel_id=1, replica_groups=mesh['seq'=8,'tp'=4] {'seq'}, use_global_device_ids=true, to_apply=%add | all-reduce | flops 32 | bytes 256
  27.8 44.8 %while.38 = (s32[]{:T(128)}, s32[1]{0:T(128)}, s32[1]{0:T(128)}, s32[1]{0:T(128)}, s32[]{:T(128)}, /*index=5*/s32[8,1]{0,1:T(1,128)S(1)}, s32[8,1]{0,1:T(1,128)S...) while((s32[]{:T(128)}, s32[1]{0:T(128)}, s32[1]{0:T(128)}, ...), condition=%wide.region_2.3_spmd, body=%wide.region_1.2_spmd.sunk | while | flops 17 | bytes 342 | solution.py:28
  79.5 3.5 %fusion.14 = f32[512]{0:T(512)S(1)} fusion(bf16[512,4608]{1,0:T(8,128)(2,1)} %all-gather.4.cloned.1.call-done), kind=kLoop, calls=%fused_computation.21 | loop fusion | flops 7077376 | bytes 4720640 | tf_op jit(solution)/shard_map/reduce_sum | solution.py:97
  90.3 4.6 %convolution_convert_fusion = bf16[512,256]{1,0:T(8,128)(2,1)S(1)} fusion(bf16[4608,256]{1,0:T(8,128)(2,1)} %param.15, bf16[512,4608]{1,0:T(8,128)(2,1)} %all-gather.4.cloned.1.call-done, f32[4608]{0:T(1024)} %param.12, f32[512]{0:T(512)S(1)} %add_rsqrt_fusion), kind=kOutput, calls=%fused_computation.29 | convolution fusion | flops 1217527808 | bytes 7360512 | tf_op jit(solution)/shard_map/dot_general | solution.py:101
  95.7 6.9 %fusion.35 = f32[512,512]{0,1:T(8,128)S(1)} fusion(bf16[4608,512]{1,0:T(8,128)(2,1)} %param.13, bf16[512,4608]{1,0:T(8,128)(2,1)} %all-gather.4.cloned.1.call-done, f32[4608]{0:T(1024)S(1)} %copy-done.11, f32[512]{0:T(512)S(1)} %add_rsqrt_fusion), kind=kOutput, calls=%fused_computation.73 | convolution fusion | flops 2425356288 | bytes 10506240 | tf_op jit(solution)/shard_map/dot_general | solution.py:99
  104.8 1.8 convert_element_type.74
  108.4 2.4 gather_fusion
  110.8 2.0 broadcast_select_fusion
  112.7 4.3 %all-to-all-start = ((bf16[4,128,2,256]{3,1,2,0:T(8,128)(2,1)}), bf16[4,128,2,256]{3,1,2,0:T(8,128)(2,1)}, u32[]{:S(2)}, u32[]{:S(2)}) async-start(bf16[4,128,2,256]{3,1,2,0:T(8,128)(2,1)} %broadcast_select_fusion), calls=%async_computation | async-start | bytes 1048576 | tf_op jit(solution)/shard_map/all_to_all | solution.py:164
  120.7 2.0 copy.86
  122.7 2.0 copy.81
  126.0 2.7 fusion.17
  128.8 2.5 fusion.19
  131.3 151.8 %while.39 = (s32[]{:T(128)}, f32[2,2,512,128]{3,2,1,0:T(8,128)}, f32[2,2,512]{2,1,0:T(2,128)S(1)}, bf16[512,2,256]{0,2,1:T(8,128)(2,1)}, s32[]{:T(128)}, /*index...) while((s32[]{:T(128)}, f32[2,2,512,128]{3,2,1,0:T(8,128)}, ...), condition=%wide.region_9.10_spmd.clone.clone, body=%wide.region_7.9_spmd.clone.clone.sunk | while | flops 547095552 | bytes 24946908 | solution.py:154
  131.3 3.4 %collective-permute-start = (bf16[512,2,256]{0,2,1:T(8,128)(2,1)}, bf16[512,2,256]{0,2,1:T(8,128)(2,1)S(1)}, u32[]{:S(2)}, u32[]{:S(2)}) collective-permute-start(bf16[512,2,256]{0,2,1:T(8,128)(2,1)} %get-tuple-element.664), channel_id=1, source_target_pairs={{0,4},{4,8},{8,12},{12,16},{16,20},{20,24},{24,28},{1,5},{5,9},{9,... | collective-permute-start | bytes 1572872 | tf_op jit(solution)/shard_map/while/body/eval_jaxpr/ppermute | solution.py:34
  135.1 13.3 %collective-permute-done = bf16[512,2,256]{0,2,1:T(8,128)(2,1)S(1)} collective-permute-done((bf16[512,2,256]{0,2,1:T(8,128)(2,1)}, bf16[512,2,256]{0,2,1:T(8,128)(2,1)S(1)}, u32[]{:S(2)}, u32[]{:S(2)}) %collective-permute-start) | collective-permute-done | bytes 524320 | tf_op jit(solution)/shard_map/while/body/eval_jaxpr/ppermute | solution.py:34
  153.2 2.5 collective-permute-start
  156.1 13.4 %collective-permute-done = bf16[512,2,256]{0,2,1:T(8,128)(2,1)S(1)} collective-permute-done((bf16[512,2,256]{0,2,1:T(8,128)(2,1)}, bf16[512,2,256]{0,2,1:T(8,128)(2,1)S(1)}, u32[]{:S(2)}, u32[]{:S(2)}) %collective-permute-start) | collective-permute-done | bytes 524320 | tf_op jit(solution)/shard_map/while/body/eval_jaxpr/ppermute | solution.py:34
  174.2 1.9 collective-permute-start
  176.6 13.0 %collective-permute-done = bf16[512,2,256]{0,2,1:T(8,128)(2,1)S(1)} collective-permute-done((bf16[512,2,256]{0,2,1:T(8,128)(2,1)}, bf16[512,2,256]{0,2,1:T(8,128)(2,1)S(1)}, u32[]{:S(2)}, u32[]{:S(2)}) %collective-permute-start) | collective-permute-done | bytes 524320 | tf_op jit(solution)/shard_map/while/body/eval_jaxpr/ppermute | solution.py:34
  194.4 1.9 collective-permute-start
  196.7 12.1 %collective-permute-done = bf16[512,2,256]{0,2,1:T(8,128)(2,1)S(1)} collective-permute-done((bf16[512,2,256]{0,2,1:T(8,128)(2,1)}, bf16[512,2,256]{0,2,1:T(8,128)(2,1)S(1)}, u32[]{:S(2)}, u32[]{:S(2)}) %collective-permute-start) | collective-permute-done | bytes 524320 | tf_op jit(solution)/shard_map/while/body/eval_jaxpr/ppermute | solution.py:34
  213.6 1.9 collective-permute-start
  215.9 11.2 %collective-permute-done = bf16[512,2,256]{0,2,1:T(8,128)(2,1)S(1)} collective-permute-done((bf16[512,2,256]{0,2,1:T(8,128)(2,1)}, bf16[512,2,256]{0,2,1:T(8,128)(2,1)S(1)}, u32[]{:S(2)}, u32[]{:S(2)}) %collective-permute-start) | collective-permute-done | bytes 524320 | tf_op jit(solution)/shard_map/while/body/eval_jaxpr/ppermute | solution.py:34
  231.9 1.9 collective-permute-start
  234.2 10.3 %collective-permute-done = bf16[512,2,256]{0,2,1:T(8,128)(2,1)S(1)} collective-permute-done((bf16[512,2,256]{0,2,1:T(8,128)(2,1)}, bf16[512,2,256]{0,2,1:T(8,128)(2,1)S(1)}, u32[]{:S(2)}, u32[]{:S(2)}) %collective-permute-start) | collective-permute-done | bytes 524320 | tf_op jit(solution)/shard_map/while/body/eval_jaxpr/ppermute | solution.py:34
  249.2 1.9 collective-permute-start
  251.5 9.9 %collective-permute-done = bf16[512,2,256]{0,2,1:T(8,128)(2,1)S(1)} collective-permute-done((bf16[512,2,256]{0,2,1:T(8,128)(2,1)}, bf16[512,2,256]{0,2,1:T(8,128)(2,1)S(1)}, u32[]{:S(2)}, u32[]{:S(2)}) %collective-permute-start) | collective-permute-done | bytes 524320 | tf_op jit(solution)/shard_map/while/body/eval_jaxpr/ppermute | solution.py:34
  266.2 1.9 collective-permute-start
  268.5 9.9 %collective-permute-done = bf16[512,2,256]{0,2,1:T(8,128)(2,1)S(1)} collective-permute-done((bf16[512,2,256]{0,2,1:T(8,128)(2,1)}, bf16[512,2,256]{0,2,1:T(8,128)(2,1)S(1)}, u32[]{:S(2)}, u32[]{:S(2)}) %collective-permute-start) | collective-permute-done | bytes 524320 | tf_op jit(solution)/shard_map/while/body/eval_jaxpr/ppermute | solution.py:34
  (171 shorter events, 84.5 us)
Async XLA Ops:
  7.2 75.8 %copy-start = (bf16[4608,256]{1,0:T(8,128)(2,1)S(1)}, bf16[4608,256]{1,0:T(8,128)(2,1)}, u32[]{:S(2)}) copy-start(bf16[4608,256]{1,0:T(8,128)(2,1)} %param.14) | copy-start | bytes 7077892
  7.2 75.8 %copy-start.10 = (f32[4608]{0:T(1024)S(1)}, f32[4608]{0:T(1024)}, u32[]{:S(2)}) copy-start(f32[4608]{0:T(1024)} %param.12) | copy-start | bytes 55300
  7.2 72.3 %all-gather.4.cloned.1.call-start = ((), (), s32[]{:S(2)}) async-start(), calls=%async_computation.1 | async-start | bytes 5898240 | tf_op jit(solution)/shard_map/all_gather | solution.py:95
  75.9 9.1 %copy-start.2 = (f32[512,64]{0,1:T(8,128)}, f32[512,64]{0,1:T(8,128)S(1)}, u32[]{:S(2)}) copy-start(f32[512,64]{0,1:T(8,128)S(1)} %get-tuple-element.493) | copy-start | bytes 393220
  79.5 3.8 %copy-start.1 = (bf16[512,4608]{1,0:T(8,128)(2,1)S(1)}, bf16[512,4608]{1,0:T(8,128)(2,1)}, u32[]{:S(2)}) copy-start(bf16[512,4608]{1,0:T(8,128)(2,1)} %all-gather.4.cloned.1.call-done) | copy-start | bytes 14155780
  90.3 5.4 %copy-start.11 = (f32[4608]{0:T(1024)S(1)}, f32[4608]{0:T(1024)}, u32[]{:S(2)}) copy-start(f32[4608]{0:T(1024)} %param.12) | copy-start | bytes 55300
  95.7 6.9 %copy-start.3 = (f32[512,64]{0,1:T(8,128)S(1)}, f32[512,64]{0,1:T(8,128)}, u32[]{:S(2)}) copy-start(f32[512,64]{0,1:T(8,128)} %copy-done.2) | copy-start | bytes 393220
  112.7 173.5 %all-to-all-start = ((bf16[4,128,2,256]{3,1,2,0:T(8,128)(2,1)}), bf16[4,128,2,256]{3,1,2,0:T(8,128)(2,1)}, u32[]{:S(2)}, u32[]{:S(2)}) async-start(bf16[4,128,2,256]{3,1,2,0:T(8,128)(2,1)} %broadcast_select_fusion), calls=%async_computation | async-start | bytes 1048576 | tf_op jit(solution)/shard_map/all_to_all | solution.py:164
  126.0 2.8 copy-start.6
  126.0 2.8 copy-start.8
  126.0 2.8 copy-start.9
  128.8 2.5 copy-start.7
  131.3 17.1 %collective-permute-start = (bf16[512,2,256]{0,2,1:T(8,128)(2,1)}, bf16[512,2,256]{0,2,1:T(8,128)(2,1)S(1)}, u32[]{:S(2)}, u32[]{:S(2)}) collective-permute-start(bf16[512,2,256]{0,2,1:T(8,128)(2,1)} %get-tuple-element.664), channel_id=1, source_target_pairs={{0,4},{4,8},{8,12},{12,16},{16,20},{20,24},{24,28},{1,5},{5,9},{9,... | collective-permute-start | bytes 1572872 | tf_op jit(solution)/shard_map/while/body/eval_jaxpr/ppermute | solution.py:34
  148.4 1.8 copy-start.4
  152.0 1.2 copy-start.5
  153.2 16.3 %collective-permute-start = (bf16[512,2,256]{0,2,1:T(8,128)(2,1)}, bf16[512,2,256]{0,2,1:T(8,128)(2,1)S(1)}, u32[]{:S(2)}, u32[]{:S(2)}) collective-permute-start(bf16[512,2,256]{0,2,1:T(8,128)(2,1)} %get-tuple-element.664), channel_id=1, source_target_pairs={{0,4},{4,8},{8,12},{12,16},{16,20},{20,24},{24,28},{1,5},{5,9},{9,... | collective-permute-start | bytes 1572872 | tf_op jit(solution)/shard_map/while/body/eval_jaxpr/ppermute | solution.py:34
  169.5 1.8 copy-start.4
  173.1 1.2 copy-start.5
  174.2 15.4 %collective-permute-start = (bf16[512,2,256]{0,2,1:T(8,128)(2,1)}, bf16[512,2,256]{0,2,1:T(8,128)(2,1)S(1)}, u32[]{:S(2)}, u32[]{:S(2)}) collective-permute-start(bf16[512,2,256]{0,2,1:T(8,128)(2,1)} %get-tuple-element.664), channel_id=1, source_target_pairs={{0,4},{4,8},{8,12},{12,16},{16,20},{20,24},{24,28},{1,5},{5,9},{9,... | collective-permute-start | bytes 1572872 | tf_op jit(solution)/shard_map/while/body/eval_jaxpr/ppermute | solution.py:34
  189.6 1.8 copy-start.4
  194.4 14.4 %collective-permute-start = (bf16[512,2,256]{0,2,1:T(8,128)(2,1)}, bf16[512,2,256]{0,2,1:T(8,128)(2,1)S(1)}, u32[]{:S(2)}, u32[]{:S(2)}) collective-permute-start(bf16[512,2,256]{0,2,1:T(8,128)(2,1)} %get-tuple-element.664), channel_id=1, source_target_pairs={{0,4},{4,8},{8,12},{12,16},{16,20},{20,24},{24,28},{1,5},{5,9},{9,... | collective-permute-start | bytes 1572872 | tf_op jit(solution)/shard_map/while/body/eval_jaxpr/ppermute | solution.py:34
  208.8 1.8 copy-start.4
  213.6 13.5 %collective-permute-start = (bf16[512,2,256]{0,2,1:T(8,128)(2,1)}, bf16[512,2,256]{0,2,1:T(8,128)(2,1)S(1)}, u32[]{:S(2)}, u32[]{:S(2)}) collective-permute-start(bf16[512,2,256]{0,2,1:T(8,128)(2,1)} %get-tuple-element.664), channel_id=1, source_target_pairs={{0,4},{4,8},{8,12},{12,16},{16,20},{20,24},{24,28},{1,5},{5,9},{9,... | collective-permute-start | bytes 1572872 | tf_op jit(solution)/shard_map/while/body/eval_jaxpr/ppermute | solution.py:34
  227.1 1.8 copy-start.4
  230.7 1.2 copy-start.5
  231.9 12.6 %collective-permute-start = (bf16[512,2,256]{0,2,1:T(8,128)(2,1)}, bf16[512,2,256]{0,2,1:T(8,128)(2,1)S(1)}, u32[]{:S(2)}, u32[]{:S(2)}) collective-permute-start(bf16[512,2,256]{0,2,1:T(8,128)(2,1)} %get-tuple-element.664), channel_id=1, source_target_pairs={{0,4},{4,8},{8,12},{12,16},{16,20},{20,24},{24,28},{1,5},{5,9},{9,... | collective-permute-start | bytes 1572872 | tf_op jit(solution)/shard_map/while/body/eval_jaxpr/ppermute | solution.py:34
  244.5 1.8 copy-start.4
  249.2 12.2 %collective-permute-start = (bf16[512,2,256]{0,2,1:T(8,128)(2,1)}, bf16[512,2,256]{0,2,1:T(8,128)(2,1)S(1)}, u32[]{:S(2)}, u32[]{:S(2)}) collective-permute-start(bf16[512,2,256]{0,2,1:T(8,128)(2,1)} %get-tuple-element.664), channel_id=1, source_target_pairs={{0,4},{4,8},{8,12},{12,16},{16,20},{20,24},{24,28},{1,5},{5,9},{9,... | collective-permute-start | bytes 1572872 | tf_op jit(solution)/shard_map/while/body/eval_jaxpr/ppermute | solution.py:34
  261.4 1.8 copy-start.4
  266.2 12.2 %collective-permute-start = (bf16[512,2,256]{0,2,1:T(8,128)(2,1)}, bf16[512,2,256]{0,2,1:T(8,128)(2,1)S(1)}, u32[]{:S(2)}, u32[]{:S(2)}) collective-permute-start(bf16[512,2,256]{0,2,1:T(8,128)(2,1)} %get-tuple-element.664), channel_id=1, source_target_pairs={{0,4},{4,8},{8,12},{12,16},{16,20},{20,24},{24,28},{1,5},{5,9},{9,... | collective-permute-start | bytes 1572872 | tf_op jit(solution)/shard_map/while/body/eval_jaxpr/ppermute | solution.py:34
  278.4 1.8 copy-start.4
  282.0 1.2 copy-start.5
  (4 other events, 4.6 us)
Sparse Core Ops, SparseCore 0:
  9.6 38.5 all-gather.3
where the time goes:
time: 297 us; the launch traced here: 296 us
  waiting for transfers between devices  93.7 us (32%)
  local copies, waits for them, and re-layouts  48 us (16%)
  matrix products  46.7 us (16%)
  loops' own time  36.2 us (12%)
  other arithmetic  23.8 us (8%)
  starting transfers between devices  21.7 us (7%)
  between operations  14.9 us (5%)
  blocking collectives  10.5 us (4%)
    ppermute x8, waiting for transfers between devices, shifted(): return lax.ppermute(block, axis, route)  93.1 us
    another operation x1, loops' own time, entering(): return lax.fori_loop(0, count - 1, hop, running)  35.6 us
    ppermute x8, starting transfers between devices, shifted(): return lax.ppermute(block, axis, route)  17.3 us
    dot_general x9, matrix products, attend_block(): jnp.einsum('qgrd,kgd->grqk', queries, keys, preferred_element_type=jnp.fl...  16.8 us
    dot_general x9, matrix products, attend_block(): jnp.einsum('grqk,kgd->grqd', weights.astype(jnp.bfloat16), values, prefer...  16.7 us
    unnamed x33, local copies, waits for them, and re-layouts  12 us
    unnamed x1, blocking collectives  10.5 us
    while x40, local copies, waits for them, and re-layouts  9.2 us
  transfers between devices with their start and end apart: 10, of which 8 were waited for; matrix products, arithmetic and copies ran while one was open for 27% of the time, Pallas kernels for 0%

commit v1 on v0

v1 whole, which is shorter than its diff:
```python
import functools
import math

import jax
import jax.numpy as jnp
from jax import lax
from jax.experimental import pallas as pl
from jax.experimental.pallas import tpu as pltpu
from jax.sharding import PartitionSpec as P

HD = 128
WIN = 4096
PAGE = 128
MESH = pl.DeviceIdType.MESH

logit_cap = 50.0
query_scale = 144.0 ** (-0.5)
norm_eps = 1e-06
SCORE_IN = query_scale / logit_cap
SCORE_OUT = logit_cap * math.log2(math.e)


def layer_kernel(
    n, back, hops, chunks,
    hidden, gain, w_query, w_key, w_value, ids_row, ids_col, freqs, table,
    attended, cache,
    hid, weights, normed, queries, own, line, pair, ids_all, numer, totals, staged, landed,
    local_sem, hid_send, hid_recv, line_send, line_recv, pair_send, pair_recv,
    ids_send, ids_recv, cache_send, cache_recv,
):
    tokens, width = hidden.shape
    model = gain.shape[1]
    q_cols, kv_cols = w_query.shape[1], w_key.shape[1]
    kv_heads = kv_cols // HD
    repeat = q_cols // kv_cols
    rows_in = tokens // chunks
    place, t = lax.axis_index("seq"), lax.axis_index("tp")
    side = place % 2
    rank = place // 2
    ranks = n // 2
    mate = place + 1 - 2 * side
    t1 = t + 1 - 2 * (t % 2)
    t2 = (t + 2) % 4
    t3 = (t1 + 2) % 4

    def rows_of(c):
        return pl.ds(pl.multiple_of(c * rows_in, rows_in), rows_in)

    def cols_of(k):
        return pl.ds(pl.multiple_of(k * width, 128), width)

    def remote(src, dst, send, recv, where):
        return pltpu.make_async_remote_copy(
            src_ref=src, dst_ref=dst, send_sem=send, recv_sem=recv,
            device_id=where, device_id_type=MESH,
        )

    loads = [
        pltpu.make_async_copy(w_query, weights.at[:, pl.ds(0, q_cols)], local_sem.at[0]),
        pltpu.make_async_copy(w_key, weights.at[:, pl.ds(q_cols, kv_cols)], local_sem.at[1]),
        pltpu.make_async_copy(
            w_value, weights.at[:, pl.ds(q_cols + kv_cols, kv_cols)], local_sem.at[2]
        ),
        pltpu.make_async_copy(hidden, hid.at[:, cols_of(t)], local_sem.at[3]),
    ]
    for load in loads:
        load.start()
    ids_all[...] = jnp.full_like(ids_all, -1)

    barrier = pltpu.get_barrier_semaphore()
    for d in range(1, back + 1):
        for other, there in ((place + d, place + d < n), (place - d, place >= d)):
            @pl.when(there)
            def _():
                pl.semaphore_signal(barrier, 1, device_id=(other, t), device_id_type=MESH)
    for k in range(1, 4):
        pl.semaphore_signal(barrier, 1, device_id=(place, (t + k) % 4), device_id_type=MESH)
    peers = 3
    for d in range(1, back + 1):
        peers = peers + jnp.where(place + d < n, 1, 0) + jnp.where(place >= d, 1, 0)
    pl.semaphore_wait(barrier, peers)

    def hid_copy(stream, c):
        rows = rows_of(c)
        if stream == 0:
            src, dst, to = hidden.at[rows], hid.at[rows, cols_of(t)], t1
        elif stream == 1:
            src, dst, to = hidden.at[rows], hid.at[rows, cols_of(t)], t2
        else:
            src, dst, to = hid.at[rows, cols_of(t2)], hid.at[rows, cols_of(t2)], t1
        return remote(src, dst, hid_send.at[stream, c], hid_recv.at[stream, c], (place, to))

    def hid_arrival(stream, c):
        rows = rows_of(c)
        dst = hid.at[rows, cols_of((t1, t2, t3)[stream])]
        return remote(dst, dst, hid_send.at[stream, c], hid_recv.at[stream, c], (place, t1))

    def ids_copy(d):
        return remote(
            ids_row, ids_all.at[d - 1], ids_send.at[d - 1], ids_recv.at[d - 1], (place + d, t)
        )

    for d in range(1, back + 1):
        @pl.when(place + d < n)
        def _():
            ids_copy(d).start()

    def first_sends(c, carry):
        hid_copy(1, c).start()
        hid_copy(0, c).start()
        return carry

    lax.fori_loop(0, chunks, first_sends, 0)

    def block_at(h, c):
        return own.at[rows_of(c)] if h == 0 else line.at[h - 1, rows_of(c)]

    def line_copy(h, c):
        return remote(
            block_at(h, c), line.at[h, rows_of(c)],
            line_send.at[h, c], line_recv.at[h, c], (place + 2, t),
        )

    def line_goes(h):
        return (rank >= h) & (rank + 1 < ranks)

    def pair_copy(h, c):
        return remote(
            block_at(h, c), pair.at[h, rows_of(c)],
            pair_send.at[h, c], pair_recv.at[h, c], (mate, t),
        )

    def pair_goes(h, at):
        reach = 2 * h + 1 - 2 * at
        return (rank >= h) & (reach > 0) & (reach <= back)

    def pass_on(h, c):
        if h < hops:
            @pl.when(line_goes(h))
            def _():
                line_copy(h, c).start()

        @pl.when(pair_goes(h, side))
        def _():
            pair_copy(h, c).start()

    def forward(h, c):
        @pl.when(rank >= h)
        def _():
            block = line.at[h - 1, rows_of(c)]
            remote(
                block, block, line_send.at[h - 1, c], line_recv.at[h - 1, c], (place, t1)
            ).wait_recv()
            pass_on(h, c)

    for d in range(1, back + 1):
        @pl.when(place >= d)
        def _():
            here = ids_all.at[d - 1]
            remote(here, here, ids_send.at[d - 1], ids_recv.at[d - 1], (place, t1)).wait_recv()

    first_id = ids_col[0:1, 0:1]
    prior = jnp.zeros((1, 1), jnp.float32)
    for d in range(back):
        same = jnp.where(ids_all[d, 0:1, :] == first_id, 1.0, 0.0)
        prior = prior + jnp.sum(same, axis=1, keepdims=True)

    for load in loads:
        load.wait()
    numer[...] = jnp.zeros_like(numer)
    totals[...] = jnp.zeros_like(totals)

    def project(c, carry):
        rows = rows_of(c)
        hid_arrival(1, c).wait_recv()
        hid_copy(2, c).start()
        ids_here = ids_col[rows, :]
        wide_ids = jnp.concatenate([ids_here] * (tokens // 128), axis=1)
        shape = (rows_in, tokens)
        earlier = lax.broadcasted_iota(jnp.int32, shape, 1) < (
            lax.broadcasted_iota(jnp.int32, shape, 0) + c * rows_in
        )
        local = jnp.where((wide_ids == ids_row[0:1, :]) & earlier, 1.0, 0.0)
        positions = jnp.sum(local, axis=1, keepdims=True) + jnp.where(
            ids_here == first_id, prior, 0.0
        )
        angles = positions * freqs[0:1, :]
        cosine = jnp.cos(angles)
        sine = jnp.sin(angles)
        sine = jnp.where(
            lax.broadcasted_iota(jnp.int32, sine.shape, 1) < HD // 2, -sine, sine
        )
        hid_arrival(0, c).wait_recv()
        hid_arrival(2, c).wait_recv()
        parts = model // width
        squares = jnp.zeros((rows_in, 1), jnp.float32)
        for k in range(parts):
            piece = hid[rows, k * width:(k + 1) * width].astype(jnp.float32)
            squares = squares + jnp.sum(piece * piece, axis=1, keepdims=True)
        scale = lax.rsqrt(squares * (1.0 / model) + norm_eps)
        for k in range(parts):
            here = slice(k * width, (k + 1) * width)
            piece = hid[rows, here].astype(jnp.float32)
            normed[:, here] = (piece * scale * gain[0:1, here]).astype(jnp.bfloat16)
        raw = jnp.dot(normed[...], weights[...], preferred_element_type=jnp.float32)

        def rotated(x):
            return (x * cosine + pltpu.roll(x, HD // 2, 1) * sine).astype(jnp.bfloat16)

        for j in range(kv_heads):
            at = q_cols + j * HD
            own[rows, j * HD:(j + 1) * HD] = rotated(raw[:, at:at + HD])
        own[rows, kv_cols:] = raw[:, q_cols + kv_cols:].astype(jnp.bfloat16)
        pass_on(0, c)
        for j in range(q_cols // HD):
            queries[j, rows, :] = rotated(raw[:, j * HD:(j + 1) * HD])
        for h in range(1, hops + 1):
            @pl.when(c >= h)
            def _():
                forward(h, c - h)
        return carry

    lax.fori_loop(0, chunks, project, 0)

    tile = min(256, tokens)

    def attend(block, id_row, causal):
        def one(step, carry):
            group, at = step // (tokens // tile), step % (tokens // tile)
            rows = pl.ds(pl.multiple_of(at * tile, tile), tile)
            keys = block[:, pl.ds(pl.multiple_of(group * HD, HD), HD)]
            values = block[:, pl.ds(pl.multiple_of(kv_cols + group * HD, HD), HD)]
            allowed = jnp.concatenate([ids_col[rows, :]] * (tokens // 128), axis=1) == id_row
            if causal:
                shape = (tile, tokens)
                allowed = allowed & (
                    lax.broadcasted_iota(jnp.int32, shape, 1)
                    <= lax.broadcasted_iota(jnp.int32, shape, 0) + at * tile
                )
            for k in range(repeat):
                head = group * repeat + k
                scores = lax.dot_general(
                    queries[head, rows, :], keys, (((1,), (1,)), ((), ())),
                    preferred_element_type=jnp.float32,
                )
                raised = jnp.exp2(SCORE_OUT * jnp.tanh(scores * SCORE_IN))
                wts = jnp.where(allowed, raised, 0.0)
                part = wts[:, :128]
                for m in range(1, tokens // 128):
                    part = part + wts[:, m * 128:(m + 1) * 128]
                totals[head, rows, :] += part
                numer[head, rows, :] += jnp.dot(
                    wts.astype(jnp.bfloat16), values, preferred_element_type=jnp.float32
                )
            return carry

        lax.fori_loop(0, kv_heads * (tokens // tile), one, 0)

    def attend_line(h):
        if 2 * h > back:
            return

        @pl.when(rank >= h)
        def _():
            attend(line.at[h - 1], ids_all[2 * h - 1, 0:1, :], False)

    def attend_pair(h):
        @pl.when(pair_goes(h, 1 - side))
        def _():
            for c in range(chunks):
                block = pair.at[h, rows_of(c)]
                remote(
                    block, block, pair_send.at[h, c], pair_recv.at[h, c], (place, t1)
                ).wait_recv()
            attend(pair.at[h], ids_all[2 * h + 2 * side - 2, 0:1, :], False)

    for j in range(chunks):
        picked = own[0:rows_in, :]
        for g in range(1, chunks):
            picked = jnp.where(table[0, g] == j, own[g * rows_in:(g + 1) * rows_in, :], picked)
        staged[j] = picked

        @pl.when(t == j)
        def _():
            landed[j] = picked

    def cache_copy(k):
        j = (t + k) % 4
        return remote(
            staged.at[j], landed.at[t], cache_send.at[k], cache_recv.at[k], (place, j)
        )

    for k in range(1, 4):
        cache_copy(k).start()

    attend(own, ids_row[0:1, :], True)
    for h in range(1, hops + 1):
        for later in range(h, hops + 1):
            for c in range(chunks):
                if c + later == chunks - 1 + h:
                    forward(later, c)
        attend_pair(h - 1)
        attend_line(h)
    attend_pair(hops)

    for head in range(q_cols // HD):
        total = jnp.sum(totals[head], axis=1, keepdims=True)
        attended[:, head * HD:(head + 1) * HD] = (numer[head] / total).astype(jnp.bfloat16)

    for k in range(1, 4):
        cache_copy(k).wait_send()
        got = landed.at[(t + 4 - k) % 4]
        remote(got, got, cache_send.at[k], cache_recv.at[k], (place, t1)).wait_recv()
    cache[...] = landed[...]

    def drain(c, carry):
        for stream in range(3):
            hid_copy(stream, c).wait_send()
        for h in range(hops + 1):
            if h < hops:
                @pl.when(line_goes(h))
                def _():
                    line_copy(h, c).wait_send()

            @pl.when(pair_goes(h, side))
            def _():
                pair_copy(h, c).wait_send()
        return carry

    lax.fori_loop(0, chunks, drain, 0)
    for d in range(1, back + 1):
        @pl.when(place + d < n)
        def _():
            ids_copy(d).wait_send()


def per_device(n, hidden, norm_gain, w_query, w_key, w_value, segment_ids, page_table):
    tokens, width = hidden.shape
    model = norm_gain.shape[0]
    q_cols, kv_cols = w_query.shape[1], w_key.shape[1]
    chunks = tokens // PAGE
    back = min(WIN // tokens, n - 1)
    hops = min(n // 2 - 1, (back + 1) // 2)
    ids_row = jnp.broadcast_to(segment_ids[None, :], (8, tokens))
    ids_col = jnp.broadcast_to(segment_ids[:, None], (tokens, 128))
    half = HD // 2
    freqs = 10000.0 ** (-(jnp.arange(half, dtype=jnp.float32) * (2.0 / HD)))
    freqs = jnp.broadcast_to(jnp.concatenate([freqs, freqs])[None, :], (8, HD))
    vmem = pl.BlockSpec(memory_space=pltpu.VMEM)
    hbm = pl.BlockSpec(memory_space=pl.ANY)
    heads = q_cols // HD
    dma = pltpu.SemaphoreType.DMA
    attended, cache = pl.pallas_call(
        functools.partial(layer_kernel, n, back, hops, chunks),
        out_shape=(
            jax.ShapeDtypeStruct((tokens, q_cols), jnp.bfloat16),
            jax.ShapeDtypeStruct((chunks, PAGE, 2 * kv_cols), jnp.bfloat16),
        ),
        in_specs=[
            vmem, vmem, hbm, hbm, hbm, vmem, vmem, vmem,
            pl.BlockSpec(memory_space=pltpu.SMEM),
        ],
        out_specs=(vmem, vmem),
        scratch_shapes=[
            pltpu.VMEM((tokens, model), jnp.bfloat16),
            pltpu.VMEM((model, q_cols + 2 * kv_cols), jnp.bfloat16),
            pltpu.VMEM((tokens // chunks, model), jnp.bfloat16),
            pltpu.VMEM((heads, tokens, HD), jnp.bfloat16),
            pltpu.VMEM((tokens, 2 * kv_cols), jnp.bfloat16),
            pltpu.VMEM((hops, tokens, 2 * kv_cols), jnp.bfloat16),
            pltpu.VMEM((hops + 1, tokens, 2 * kv_cols), jnp.bfloat16),
            pltpu.VMEM((back, 8, tokens), jnp.int32),
            pltpu.VMEM((heads, tokens, HD), jnp.float32),
            pltpu.VMEM((heads, tokens, 128), jnp.float32),
            pltpu.VMEM((chunks, PAGE, 2 * kv_cols), jnp.bfloat16),
            pltpu.VMEM((chunks, PAGE, 2 * kv_cols), jnp.bfloat16),
            dma((4,)),
            dma((3, chunks)), dma((3, chunks)),
            dma((hops, chunks)), dma((hops, chunks)),
            dma((hops + 1, chunks)), dma((hops + 1, chunks)),
            dma((back,)), dma((back,)),
            dma((4,)), dma((4,)),
        ],
        compiler_params=pltpu.CompilerParams(
            collective_id=0, has_side_effects=True, vmem_limit_bytes=56 * 1024 * 1024
        ),
        cost_estimate=pl.CostEstimate(
            flops=2 * tokens * model * (q_cols + 2 * kv_cols)
            + 4 * heads * tokens * HD * tokens * (back + 1),
            bytes_accessed=2 * model * (q_cols + 2 * kv_cols),
            transcendentals=2 * heads * tokens * tokens * (back + 1),
        ),
    )(
        hidden, norm_gain[None, :], w_query, w_key, w_value, ids_row, ids_col, freqs, page_table
    )
    pages = cache.reshape(chunks, PAGE, 2, kv_cols)
    kv_cache = jnp.transpose(pages, (1, 2, 0, 3)).reshape(1, PAGE, 2, chunks * kv_cols)
    return (attended, kv_cache)


def solution(mesh):
    placed = (
        P("seq", "tp"),
        P(),
        P(None, "tp"),
        P(None, "tp"),
        P(None, "tp"),
        P("seq"),
        P("seq", None),
    )
    return jax.shard_map(
        functools.partial(per_device, mesh.shape["seq"]),
        mesh=mesh,
        in_specs=placed,
        out_specs=(P("seq", "tp"), P(("seq", "tp"), None, None, None)),
        check_vma=False,
    )
```

time: 297 us -> 81.6 us (0.27)
  the two profiles are of different devices: /device:TPU:8 before, /device:TPU:27 now
where the time goes in v1:
time: 81.6 us; the launch traced here: 81.3 us
  Pallas kernels  72.1 us (88%)
  local copies, waits for them, and re-layouts  8.43 us (10%)
    pallas_call x1, Pallas kernels, per_device(): pl.pallas_call(functools.partial(layer_kernel, n, back, hops, chunks), ou...  72.1 us

profile of v1, /device:TPU:27, one launch (start us, length us, event | category | flops | bytes accessed | tf_op | source)
XLA Modules:
  0.0 81.3 jit_solution(1190130959898579590)
XLA Ops:
  0.6 0.1 pad_maximum_fusion
  0.7 0.6 broadcast_in_dim.11.freqs
  1.3 1.3 %broadcast_in_dim.9.ids_row = s32[8,512]{1,0:T(8,128)} broadcast(s32[512]{0:T(512)} %param.12), dimensions={1} | broadcast | bytes 18432 | tf_op jit(solution)/shard_map/broadcast_in_dim | solution.py:344
  2.6 1.3 %broadcast_in_dim.8.gain = f32[1,4608]{1,0:T(1,128)} reshape(f32[4608]{0:T(1024)} %param.8) | data formatting | bytes 36864 | tf_op jit(solution)/shard_map/broadcast_in_dim | solution.py:394
  3.9 1.5 %broadcast_in_dim.10.ids_col = s32[512,128]{1,0:T(8,128)} broadcast(s32[512]{0:T(512)} %param.12), dimensions={0} | broadcast | bytes 264192 | tf_op jit(solution)/shard_map/broadcast_in_dim | solution.py:345
  5.5 72.1 %shard_map.86 = (bf16[512,512]{1,0:T(8,128)(2,1)}, bf16[4,128,512]{2,1,0:T(8,128)(2,1)}) custom-call(bf16[512,1152]{1,0:T(8,128)(2,1)} %hidden.1, f32[1,4608]{1,0:T(1,128)} %broadcast_in_dim.8.gain, bf16[4608,512]{1,0:T(8,128)(2,1)} %w_query.1, bf16[4608,256]{1,0:T(8,128)(2,1)} %w_key.1, bf16[4608,256]{1,0:T(8,128)(2,1)} %w_value.1, ...), custom_call_target="tpu_custom_call" | custom-call | flops 9126805504 | bytes 9437184 | tf_op jit(solution)/shard_map/pallas_call | solution.py:353
  77.6 0.0 copy-start
  77.6 1.2 %reshape.13 = bf16[4,128,2,256]{3,2,1,0:T(2,128)(2,1)S(1)} reshape(bf16[4,128,512]{2,1,0:T(8,128)(2,1)} %get-tuple-element.5) | data formatting | bytes 1048576 | tf_op jit(solution)/shard_map/reshape | solution.py:396
  78.8 0.7 copy.9
  79.5 1.0 %reshape.14 = bf16[1,128,2,1024]{3,2,1,0:T(2,128)(2,1)} reshape(bf16[128,2,4,256]{3,2,1,0:T(4,128)(2,1)S(1)} %copy.9) | data formatting | bytes 1048576 | tf_op jit(solution)/shard_map/reshape | solution.py:397
  80.5 0.0 copy-done
  80.5 0.8 copy.11
  (1 shorter events, 0.0 us)
Async XLA Ops:
  77.6 2.9 %copy-start = (bf16[512,512]{1,0:T(8,128)(2,1)S(1)}, bf16[512,512]{1,0:T(8,128)(2,1)}, u32[]{:S(2)}) copy-start(bf16[512,512]{1,0:T(8,128)(2,1)} %get-tuple-element.8) | copy-start | bytes 1572868

commit v2 on v1

--- a/solution.py
+++ b/solution.py
@@ -3,6 +3,7 @@
 
 import jax
 import jax.numpy as jnp
+import numpy as np
 from jax import lax
 from jax.experimental import pallas as pl
 from jax.experimental.pallas import tpu as pltpu
@@ -22,8 +23,9 @@
 
 def layer_kernel(
     n, back, hops, chunks,
-    hidden, gain, w_query, w_key, w_value, ids_row, ids_col, freqs, table,
+    hidden, gain_flat, w_query, w_key, w_value, ids_flat, freqs, table,
     attended, cache,
+    gain, ids_row, ids_col, cosines, sines, woven,
     hid, weights, normed, queries, own, line, pair, ids_all, numer, totals, staged, landed,
     local_sem, hid_send, hid_recv, line_send, line_recv, pair_send, pair_recv,
     ids_send, ids_recv, cache_send, cache_recv,
@@ -66,6 +68,7 @@
     for load in loads:
         load.start()
     ids_all[...] = jnp.full_like(ids_all, -1)
+    ids_row[...] = jnp.broadcast_to(ids_flat[...].reshape(1, tokens), (8, tokens))
 
     barrier = pltpu.get_barrier_semaphore()
     for d in range(1, back + 1):
@@ -159,21 +162,19 @@
             here = ids_all.at[d - 1]
             remote(here, here, ids_send.at[d - 1], ids_recv.at[d - 1], (place, t1)).wait_recv()
 
+    gain[...] = jnp.broadcast_to(gain_flat[...].reshape(1, model), gain.shape)
+    for c in range(tokens // 128):
+        here = slice(c * 128, (c + 1) * 128)
+        spread = jnp.broadcast_to(ids_row[0:1, here].astype(jnp.float32), (128, 128))
+        ids_col[here, :] = jnp.transpose(spread).astype(jnp.int32)
     first_id = ids_col[0:1, 0:1]
     prior = jnp.zeros((1, 1), jnp.float32)
     for d in range(back):
         same = jnp.where(ids_all[d, 0:1, :] == first_id, 1.0, 0.0)
         prior = prior + jnp.sum(same, axis=1, keepdims=True)
 
-    for load in loads:
-        load.wait()
-    numer[...] = jnp.zeros_like(numer)
-    totals[...] = jnp.zeros_like(totals)
-
-    def project(c, carry):
+    def prepare(c, carry):
         rows = rows_of(c)
-        hid_arrival(1, c).wait_recv()
-        hid_copy(2, c).start()
         ids_here = ids_col[rows, :]
         wide_ids = jnp.concatenate([ids_here] * (tokens // 128), axis=1)
         shape = (rows_in, tokens)
@@ -185,24 +186,65 @@
             ids_here == first_id, prior, 0.0
         )
         angles = positions * freqs[0:1, :]
-        cosine = jnp.cos(angles)
         sine = jnp.sin(angles)
-        sine = jnp.where(
+        cosines[rows, :] = jnp.cos(angles)
+        sines[rows, :] = jnp.where(
             lax.broadcasted_iota(jnp.int32, sine.shape, 1) < HD // 2, -sine, sine
         )
+        return carry
+
+    lax.fori_loop(0, chunks, prepare, 0)
+    numer[...] = jnp.zeros_like(numer)
+    totals[...] = jnp.zeros_like(totals)
+    own[...] = jnp.zeros_like(own)
+    for load in loads:
+        load.wait()
+
+    def attend_tile(block, id_row, group, at, size, causal):
+        rows = pl.ds(pl.multiple_of(at * size, size), size)
+        keys = block[:, pl.ds(pl.multiple_of(group * HD, HD), HD)]
+        values = block[:, pl.ds(pl.multiple_of(kv_cols + group * HD, HD), HD)]
+        allowed = jnp.concatenate([ids_col[rows, :]] * (tokens // 128), axis=1) == id_row
+        if causal:
+            shape = (size, tokens)
+            allowed = allowed & (
+                lax.broadcasted_iota(jnp.int32, shape, 1)
+                <= lax.broadcasted_iota(jnp.int32, shape, 0) + at * size
+            )
+        for k in range(repeat):
+            head = group * repeat + k
+            scores = lax.dot_general(
+                queries[head, rows, :], keys, (((1,), (1,)), ((), ())),
+                preferred_element_type=jnp.float32,
+            )
+            raised = jnp.exp2(SCORE_OUT * jnp.tanh(scores * SCORE_IN))
+            wts = jnp.where(allowed, raised, 0.0)
+            part = wts[:, :128]
+            for m in range(1, tokens // 128):
+                part = part + wts[:, m * 128:(m + 1) * 128]
+            totals[head, rows, :] += part
+            numer[head, rows, :] += jnp.dot(
+                wts.astype(jnp.bfloat16), values, preferred_element_type=jnp.float32
+            )
+
+    def project(c, carry):
+        rows = rows_of(c)
+        hid_arrival(1, c).wait_recv()
+        hid_copy(2, c).start()
         hid_arrival(0, c).wait_recv()
-        hid_arrival(2, c).wait_recv()
-        parts = model // width
         squares = jnp.zeros((rows_in, 1), jnp.float32)
-        for k in range(parts):
-            piece = hid[rows, k * width:(k + 1) * width].astype(jnp.float32)
+        for k in (t, t1, t2, t3):
+            if k is t3:
+                hid_arrival(2, c).wait_recv()
+            piece = hid[rows, cols_of(k)].astype(jnp.float32)
             squares = squares + jnp.sum(piece * piece, axis=1, keepdims=True)
         scale = lax.rsqrt(squares * (1.0 / model) + norm_eps)
-        for k in range(parts):
+        for k in range(model // width):
             here = slice(k * width, (k + 1) * width)
             piece = hid[rows, here].astype(jnp.float32)
             normed[:, here] = (piece * scale * gain[0:1, here]).astype(jnp.bfloat16)
         raw = jnp.dot(normed[...], weights[...], preferred_element_type=jnp.float32)
+        cosine, sine = cosines[rows, :], sines[rows, :]
 
         def rotated(x):
             return (x * cosine + pltpu.roll(x, HD // 2, 1) * sine).astype(jnp.bfloat16)
@@ -214,6 +256,8 @@
         pass_on(0, c)
         for j in range(q_cols // HD):
             queries[j, rows, :] = rotated(raw[:, j * HD:(j + 1) * HD])
+        for group in range(kv_heads):
+            attend_tile(own, ids_row[0:1, :], group, c, rows_in, True)
         for h in range(1, hops + 1):
             @pl.when(c >= h)
             def _():
@@ -224,34 +268,10 @@
 
     tile = min(256, tokens)
 
-    def attend(block, id_row, causal):
+    def attend(block, id_row):
         def one(step, carry):
             group, at = step // (tokens // tile), step % (tokens // tile)
-            rows = pl.ds(pl.multiple_of(at * tile, tile), tile)
-            keys = block[:, pl.ds(pl.multiple_of(group * HD, HD), HD)]
-            values = block[:, pl.ds(pl.multiple_of(kv_cols + group * HD, HD), HD)]
-            allowed = jnp.concatenate([ids_col[rows, :]] * (tokens // 128), axis=1) == id_row
-            if causal:
-                shape = (tile, tokens)
-                allowed = allowed & (
-                    lax.broadcasted_iota(jnp.int32, shape, 1)
-                    <= lax.broadcasted_iota(jnp.int32, shape, 0) + at * tile
-                )
-            for k in range(repeat):
-                head = group * repeat + k
-                scores = lax.dot_general(
-                    queries[head, rows, :], keys, (((1,), (1,)), ((), ())),
-                    preferred_element_type=jnp.float32,
-                )
-                raised = jnp.exp2(SCORE_OUT * jnp.tanh(scores * SCORE_IN))
-                wts = jnp.where(allowed, raised, 0.0)
-                part = wts[:, :128]
-                for m in range(1, tokens // 128):
-                    part = part + wts[:, m * 128:(m + 1) * 128]
-                totals[head, rows, :] += part
-                numer[head, rows, :] += jnp.dot(
-                    wts.astype(jnp.bfloat16), values, preferred_element_type=jnp.float32
-                )
+            attend_tile(block, id_row, group, at, tile, False)
             return carry
 
         lax.fori_loop(0, kv_heads * (tokens // tile), one, 0)
@@ -262,7 +282,7 @@
 
         @pl.when(rank >= h)
         def _():
-            attend(line.at[h - 1], ids_all[2 * h - 1, 0:1, :], False)
+            attend(line.at[h - 1], ids_all[2 * h - 1, 0:1, :])
 
     def attend_pair(h):
         @pl.when(pair_goes(h, 1 - side))
@@ -272,7 +292,7 @@
                 remote(
                     block, block, pair_send.at[h, c], pair_recv.at[h, c], (place, t1)
                 ).wait_recv()
-            attend(pair.at[h], ids_all[2 * h + 2 * side - 2, 0:1, :], False)
+            attend(pair.at[h], ids_all[2 * h + 2 * side - 2, 0:1, :])
 
     for j in range(chunks):
         picked = own[0:rows_in, :]
@@ -293,15 +313,18 @@
     for k in range(1, 4):
         cache_copy(k).start()
 
-    attend(own, ids_row[0:1, :], True)
+    waiting = [("pair", 0)]
+    for h in range(1, hops + 1):
+        waiting += [("line", h), ("pair", h)]
+    ready = 0
     for h in range(1, hops + 1):
         for later in range(h, hops + 1):
-            for c in range(chunks):
-                if c + later == chunks - 1 + h:
-                    forward(later, c)
-        attend_pair(h - 1)
-        attend_line(h)
-    attend_pair(hops)
+            forward(later, chunks - 1 + h - later)
+        kind, index = waiting[ready]
+        (attend_pair if kind == "pair" else attend_line)(index)
+        ready += 1
+    for kind, index in waiting[ready:]:
+        (attend_pair if kind == "pair" else attend_line)(index)
 
     for head in range(q_cols // HD):
         total = jnp.sum(totals[head], axis=1, keepdims=True)
@@ -311,7 +334,14 @@
         cache_copy(k).wait_send()
         got = landed.at[(t + 4 - k) % 4]
         remote(got, got, cache_send.at[k], cache_recv.at[k], (place, t1)).wait_recv()
-    cache[...] = landed[...]
+    for k in range(chunks):
+        for part in range(2):
+            got = landed[k, :, part * kv_cols:(part + 1) * kv_cols].astype(jnp.float32)
+            for m in range(kv_cols // 128):
+                at = k * (kv_cols // 128) + m
+                woven[at, pl.ds(part, PAGE, stride=2), :] = got[:, m * 128:(m + 1) * 128]
+    for at in range(chunks * kv_cols // 128):
+        cache[:, at * 128:(at + 1) * 128] = woven[at].astype(jnp.bfloat16)
 
     def drain(c, carry):
         for stream in range(3):
@@ -341,11 +371,9 @@
     chunks = tokens // PAGE
     back = min(WIN // tokens, n - 1)
     hops = min(n // 2 - 1, (back + 1) // 2)
-    ids_row = jnp.broadcast_to(segment_ids[None, :], (8, tokens))
-    ids_col = jnp.broadcast_to(segment_ids[:, None], (tokens, 128))
     half = HD // 2
-    freqs = 10000.0 ** (-(jnp.arange(half, dtype=jnp.float32) * (2.0 / HD)))
-    freqs = jnp.broadcast_to(jnp.concatenate([freqs, freqs])[None, :], (8, HD))
+    freqs = np.power(np.float32(10000.0), -(np.arange(half, dtype=np.float32) * np.float32(2.0 / HD)))
+    freqs = np.tile(np.concatenate([freqs, freqs])[None, :], (8, 1)).astype(np.float32)
     vmem = pl.BlockSpec(memory_space=pltpu.VMEM)
     hbm = pl.BlockSpec(memory_space=pl.ANY)
     heads = q_cols // HD
@@ -354,14 +382,20 @@
         functools.partial(layer_kernel, n, back, hops, chunks),
         out_shape=(
             jax.ShapeDtypeStruct((tokens, q_cols), jnp.bfloat16),
-            jax.ShapeDtypeStruct((chunks, PAGE, 2 * kv_cols), jnp.bfloat16),
+            jax.ShapeDtypeStruct((2 * PAGE, chunks * kv_cols), jnp.bfloat16),
         ),
         in_specs=[
-            vmem, vmem, hbm, hbm, hbm, vmem, vmem, vmem,
+            vmem, vmem, hbm, hbm, hbm, vmem, vmem,
             pl.BlockSpec(memory_space=pltpu.SMEM),
         ],
         out_specs=(vmem, vmem),
         scratch_shapes=[
+            pltpu.VMEM((8, model), jnp.float32),
+            pltpu.VMEM((8, tokens), jnp.int32),
+            pltpu.VMEM((tokens, 128), jnp.int32),
+            pltpu.VMEM((tokens, HD), jnp.float32),
+            pltpu.VMEM((tokens, HD), jnp.float32),
+            pltpu.VMEM((chunks * kv_cols // 128, 2 * PAGE, 128), jnp.float32),
             pltpu.VMEM((tokens, model), jnp.bfloat16),
             pltpu.VMEM((model, q_cols + 2 * kv_cols), jnp.bfloat16),
             pltpu.VMEM((tokens // chunks, model), jnp.bfloat16),
@@ -391,10 +425,9 @@
             transcendentals=2 * heads * tokens * tokens * (back + 1),
         ),
     )(
-        hidden, norm_gain[None, :], w_query, w_key, w_value, ids_row, ids_col, freqs, page_table
+        hidden, norm_gain, w_query, w_key, w_value, segment_ids, freqs, page_table
     )
-    pages = cache.reshape(chunks, PAGE, 2, kv_cols)
-    kv_cache = jnp.transpose(pages, (1, 2, 0, 3)).reshape(1, PAGE, 2, chunks * kv_cols)
+    kv_cache = cache.reshape(1, PAGE, 2, chunks * kv_cols)
     return (attended, kv_cache)
 
 

time: 81.6 us -> 78.2 us (0.958); the launches traced: 81.3 us -> 77 us
  local copies, waits for them, and re-layouts: 8.43 us -> 3.9 us
    broadcast_in_dim x4 -> x0, local copies, waits for them, and re-layouts: 4.74 us -> none  [the longest x1 1.52 us: per_device(): ids_col = jnp.broadcast_to(segment_ids[:, None], (tokens, 128))]
    unnamed x3 -> x1, local copies, waits for them, and re-layouts: 0.8 us -> 1.87 us
    reshape x2 -> x1, local copies, waits for them, and re-layouts: 2.21 us -> 2.03 us  [per_device(): kv_cache = cache.reshape(1, PAGE, 2, chunks * kv_cols)]
where the time goes in v2:
time: 78.2 us; the launch traced here: 77 us
  Pallas kernels  72.5 us (93%)
  local copies, waits for them, and re-layouts  3.9 us (5%)
    pallas_call x1, Pallas kernels, per_device(): pl.pallas_call(functools.partial(layer_kernel, n, back, hops, chunks), ou...  72.5 us
    reshape x1, local copies, waits for them, and re-layouts, per_device(): kv_cache = cache.reshape(1, PAGE, 2, chunks * kv_cols)  2.03 us
    unnamed x1, local copies, waits for them, and re-layouts  1.87 us

profile of v2, /device:TPU:27, one launch (start us, length us, event | category | flops | bytes accessed | tf_op | source)
XLA Modules:
  0.0 77.0 jit_solution(15886063565584182047)
XLA Ops:
  0.6 72.5 %shard_map.95 = (bf16[512,512]{1,0:T(8,128)(2,1)}, bf16[256,1024]{1,0:T(8,128)(2,1)}) custom-call(bf16[512,1152]{1,0:T(8,128)(2,1)} %hidden.1, f32[4608]{0:T(1024)} %gain_flat.1, bf16[4608,512]{1,0:T(8,128)(2,1)} %w_query.1, bf16[4608,256]{1,0:T(8,128)(2,1)} %w_key.1, bf16[4608,256]{1,0:T(8,128)(2,1)} %w_value.1, s32[512]{0:T(512)} %ids_flat.1, ...), custom_call_target="tpu_custom_call" | custom-call | flops 9126805504 | bytes 9437184 | tf_op jit(solution)/shard_map/pallas_call | solution.py:381
  73.1 2.0 %reshape.7 = bf16[1,128,2,1024]{3,2,1,0:T(2,128)(2,1)} reshape(bf16[256,1024]{1,0:T(8,128)(2,1)} %get-tuple-element.5) | data formatting | bytes 1048576 | tf_op jit(solution)/shard_map/reshape | solution.py:430
  75.2 1.9 %copy.11 = bf16[512,512]{1,0:T(8,128)(2,1)} copy(bf16[512,512]{1,0:T(8,128)(2,1)} %get-tuple-element.8) | data formatting | bytes 1048576

commit v3 on v2

--- a/solution.py
+++ b/solution.py
@@ -17,18 +17,19 @@
 logit_cap = 50.0
 query_scale = 144.0 ** (-0.5)
 norm_eps = 1e-06
+CHUNKS = 4
 SCORE_IN = query_scale / logit_cap
 SCORE_OUT = logit_cap * math.log2(math.e)
 
 
 def layer_kernel(
-    n, back, hops, chunks,
+    n, back, hops, pages, chunks,
     hidden, gain_flat, w_query, w_key, w_value, ids_flat, freqs, table,
     attended, cache,
-    gain, ids_row, ids_col, cosines, sines, woven,
+    gain, ids_row, ids_col, cosines, sines, woven, squares_own, squares_in, scales, raw_near, near,
     hid, weights, normed, queries, own, line, pair, ids_all, numer, totals, staged, landed,
     local_sem, hid_send, hid_recv, line_send, line_recv, pair_send, pair_recv,
-    ids_send, ids_recv, cache_send, cache_recv,
+    ids_send, ids_recv, cache_send, cache_recv, sq_send, sq_recv, relay_send,
 ):
     tokens, width = hidden.shape
     model = gain.shape[1]
@@ -36,6 +37,7 @@
     kv_heads = kv_cols // HD
     repeat = q_cols // kv_cols
     rows_in = tokens // chunks
+    half = 2 * width
     place, t = lax.axis_index("seq"), lax.axis_index("tp")
     side = place % 2
     rank = place // 2
@@ -70,6 +72,15 @@
     ids_all[...] = jnp.full_like(ids_all, -1)
     ids_row[...] = jnp.broadcast_to(ids_flat[...].reshape(1, tokens), (8, tokens))
 
+    def upright(row):
+        return jnp.transpose(jnp.broadcast_to(row, (128, 128)))
+
+    for c in range(tokens // 128):
+        here = slice(c * 128, (c + 1) * 128)
+        piece = hidden[here, :].astype(jnp.float32)
+        sums = jnp.sum(piece * piece, axis=1, keepdims=True)
+        squares_own[:, here] = jnp.transpose(jnp.broadcast_to(sums, (128, 128)))[0:8, :]
+
     barrier = pltpu.get_barrier_semaphore()
     for d in range(1, back + 1):
         for other, there in ((place + d, place + d < n), (place - d, place >= d)):
@@ -108,6 +119,14 @@
         def _():
             ids_copy(d).start()
 
+    def squares_copy(k):
+        return remote(
+            squares_own, squares_in.at[t], sq_send.at[k], sq_recv.at[k], (place, (t + k) % 4)
+        )
+
+    for k in range(1, 4):
+        squares_copy(k).start()
+
     def first_sends(c, carry):
         hid_copy(1, c).start()
         hid_copy(0, c).start()
@@ -136,6 +155,28 @@
     def pair_goes(h, at):
         reach = 2 * h + 1 - 2 * at
         return (rank >= h) & (reach > 0) & (reach <= back)
+
+    def direct(h, c):
+        return (side == 1) | (c % 2 == 0) if h == 1 else True
+
+    def relay_copy(c):
+        return remote(
+            pair.at[0, rows_of(c)], pair.at[1, rows_of(c)],
+            relay_send.at[c], pair_recv.at[1, c], (place + 2, t),
+        )
+
+    def relays(c):
+        return (side == 1) & (rank + 1 < ranks) & (c % 2 == 1)
+
+    def pair_wait(h, c):
+        block = pair.at[h, rows_of(c)]
+        remote(block, block, pair_send.at[h, c], pair_recv.at[h, c], (place, t1)).wait_recv()
+
+    def relay(c):
+        @pl.when(relays(c))
+        def _():
+            pair_wait(0, c)
+            relay_copy(c).start()
 
     def pass_on(h, c):
         if h < hops:
@@ -143,7 +184,7 @@
             def _():
                 line_copy(h, c).start()
 
-        @pl.when(pair_goes(h, side))
+        @pl.when(pair_goes(h, side) & direct(h, c))
         def _():
             pair_copy(h, c).start()
 
@@ -165,8 +206,7 @@
     gain[...] = jnp.broadcast_to(gain_flat[...].reshape(1, model), gain.shape)
     for c in range(tokens // 128):
         here = slice(c * 128, (c + 1) * 128)
-        spread = jnp.broadcast_to(ids_row[0:1, here].astype(jnp.float32), (128, 128))
-        ids_col[here, :] = jnp.transpose(spread).astype(jnp.int32)
+        ids_col[here, :] = upright(ids_row[0:1, here].astype(jnp.float32)).astype(jnp.int32)
     first_id = ids_col[0:1, 0:1]
     prior = jnp.zeros((1, 1), jnp.float32)
     for d in range(back):
@@ -197,8 +237,40 @@
     numer[...] = jnp.zeros_like(numer)
     totals[...] = jnp.zeros_like(totals)
     own[...] = jnp.zeros_like(own)
+    for k in range(1, 4):
+        got = squares_in.at[(t + 4 - k) % 4]
+        remote(got, got, sq_send.at[k], sq_recv.at[k], (place, t1)).wait_recv()
+    squares = squares_own[0:1, :]
+    for k in (t1, t2, t3):
+        squares = squares + squares_in[k, 0:1, :]
+    scale_row = lax.rsqrt(squares * (1.0 / model) + norm_eps)
+    for c in range(tokens // 128):
+        here = slice(c * 128, (c + 1) * 128)
+        scales[here, :] = upright(scale_row[:, here])
     for load in loads:
         load.wait()
+    near_cols = pl.ds(pl.multiple_of((t // 2) * half, 128), half)
+    far_cols = pl.ds(pl.multiple_of((1 - t // 2) * half, 128), half)
+
+    def normalized(rows, cols):
+        piece = hid[rows, cols].astype(jnp.float32)
+        return (piece * scales[rows, 0:1] * gain[0:1, cols]).astype(jnp.bfloat16)
+
+    def near_norm(c, carry):
+        hid_arrival(0, c).wait_recv()
+        near[rows_of(c), :] = normalized(rows_of(c), near_cols)
+        return carry
+
+    lax.fori_loop(0, chunks, near_norm, 0)
+
+    def near_dot(j, carry):
+        cols = pl.ds(pl.multiple_of(j * 256, 256), 256)
+        raw_near[:, cols] = jnp.dot(
+            near[...], weights[near_cols, cols], preferred_element_type=jnp.float32
+        )
+        return carry
+
+    lax.fori_loop(0, weights.shape[1] // 256, near_dot, 0)
 
     def attend_tile(block, id_row, group, at, size, causal):
         rows = pl.ds(pl.multiple_of(at * size, size), size)
@@ -231,19 +303,11 @@
         rows = rows_of(c)
         hid_arrival(1, c).wait_recv()
         hid_copy(2, c).start()
-        hid_arrival(0, c).wait_recv()
-        squares = jnp.zeros((rows_in, 1), jnp.float32)
-        for k in (t, t1, t2, t3):
-            if k is t3:
-                hid_arrival(2, c).wait_recv()
-            piece = hid[rows, cols_of(k)].astype(jnp.float32)
-            squares = squares + jnp.sum(piece * piece, axis=1, keepdims=True)
-        scale = lax.rsqrt(squares * (1.0 / model) + norm_eps)
-        for k in range(model // width):
-            here = slice(k * width, (k + 1) * width)
-            piece = hid[rows, here].astype(jnp.float32)
-            normed[:, here] = (piece * scale * gain[0:1, here]).astype(jnp.bfloat16)
-        raw = jnp.dot(normed[...], weights[...], preferred_element_type=jnp.float32)
+        hid_arrival(2, c).wait_recv()
+        normed[...] = normalized(rows, far_cols)
+        raw = raw_near[rows, :] + jnp.dot(
+            normed[...], weights[far_cols, :], preferred_element_type=jnp.float32
+        )
         cosine, sine = cosines[rows, :], sines[rows, :]
 
         def rotated(x):
@@ -258,6 +322,9 @@
             queries[j, rows, :] = rotated(raw[:, j * HD:(j + 1) * HD])
         for group in range(kv_heads):
             attend_tile(own, ids_row[0:1, :], group, c, rows_in, True)
+        @pl.when(c >= 1)
+        def _():
+            relay(c - 1)
         for h in range(1, hops + 1):
             @pl.when(c >= h)
             def _():
@@ -288,16 +355,19 @@
         @pl.when(pair_goes(h, 1 - side))
         def _():
             for c in range(chunks):
-                block = pair.at[h, rows_of(c)]
-                remote(
-                    block, block, pair_send.at[h, c], pair_recv.at[h, c], (place, t1)
-                ).wait_recv()
+                if h == 0:
+                    @pl.when(jnp.logical_not(relays(c)))
+                    def _():
+                        pair_wait(0, c)
+                else:
+                    pair_wait(h, c)
             attend(pair.at[h], ids_all[2 * h + 2 * side - 2, 0:1, :])
 
-    for j in range(chunks):
-        picked = own[0:rows_in, :]
-        for g in range(1, chunks):
-            picked = jnp.where(table[0, g] == j, own[g * rows_in:(g + 1) * rows_in, :], picked)
+    relay(chunks - 1)
+    for j in range(pages):
+        picked = own[0:PAGE, :]
+        for g in range(1, pages):
+            picked = jnp.where(table[0, g] == j, own[g * PAGE:(g + 1) * PAGE, :], picked)
         staged[j] = picked
 
         @pl.when(t == j)
@@ -332,15 +402,16 @@
 
     for k in range(1, 4):
         cache_copy(k).wait_send()
+        squares_copy(k).wait_send()
         got = landed.at[(t + 4 - k) % 4]
         remote(got, got, cache_send.at[k], cache_recv.at[k], (place, t1)).wait_recv()
-    for k in range(chunks):
+    for k in range(pages):
         for part in range(2):
             got = landed[k, :, part * kv_cols:(part + 1) * kv_cols].astype(jnp.float32)
             for m in range(kv_cols // 128):
                 at = k * (kv_cols // 128) + m
                 woven[at, pl.ds(part, PAGE, stride=2), :] = got[:, m * 128:(m + 1) * 128]
-    for at in range(chunks * kv_cols // 128):
+    for at in range(pages * kv_cols // 128):
         cache[:, at * 128:(at + 1) * 128] = woven[at].astype(jnp.bfloat16)
 
     def drain(c, carry):
@@ -352,9 +423,13 @@
                 def _():
                     line_copy(h, c).wait_send()
 
-            @pl.when(pair_goes(h, side))
+            @pl.when(pair_goes(h, side) & direct(h, c))
             def _():
                 pair_copy(h, c).wait_send()
+
+        @pl.when(relays(c))
+        def _():
+            relay_copy(c).wait_send()
         return carry
 
     lax.fori_loop(0, chunks, drain, 0)
@@ -368,7 +443,8 @@
     tokens, width = hidden.shape
     model = norm_gain.shape[0]
     q_cols, kv_cols = w_query.shape[1], w_key.shape[1]
-    chunks = tokens // PAGE
+    pages = tokens // PAGE
+    chunks = CHUNKS
     back = min(WIN // tokens, n - 1)
     hops = min(n // 2 - 1, (back + 1) // 2)
     half = HD // 2
@@ -379,10 +455,10 @@
     heads = q_cols // HD
     dma = pltpu.SemaphoreType.DMA
     attended, cache = pl.pallas_call(
-        functools.partial(layer_kernel, n, back, hops, chunks),
+        functools.partial(layer_kernel, n, back, hops, pages, chunks),
         out_shape=(
             jax.ShapeDtypeStruct((tokens, q_cols), jnp.bfloat16),
-            jax.ShapeDtypeStruct((2 * PAGE, chunks * kv_cols), jnp.bfloat16),
+            jax.ShapeDtypeStruct((2 * PAGE, pages * kv_cols), jnp.bfloat16),
         ),
         in_specs=[
             vmem, vmem, hbm, hbm, hbm, vmem, vmem,
@@ -395,10 +471,15 @@
             pltpu.VMEM((tokens, 128), jnp.int32),
             pltpu.VMEM((tokens, HD), jnp.float32),
             pltpu.VMEM((tokens, HD), jnp.float32),
-            pltpu.VMEM((chunks * kv_cols // 128, 2 * PAGE, 128), jnp.float32),
+            pltpu.VMEM((pages * kv_cols // 128, 2 * PAGE, 128), jnp.float32),
+            pltpu.VMEM((8, tokens), jnp.float32),
+            pltpu.VMEM((4, 8, tokens), jnp.float32),
+            pltpu.VMEM((tokens, 128), jnp.float32),
+            pltpu.VMEM((tokens, q_cols + 2 * kv_cols), jnp.float32),
+            pltpu.VMEM((tokens, 2 * width), jnp.bfloat16),
             pltpu.VMEM((tokens, model), jnp.bfloat16),
             pltpu.VMEM((model, q_cols + 2 * kv_cols), jnp.bfloat16),
-            pltpu.VMEM((tokens // chunks, model), jnp.bfloat16),
+            pltpu.VMEM((tokens // chunks, 2 * width), jnp.bfloat16),
             pltpu.VMEM((heads, tokens, HD), jnp.bfloat16),
             pltpu.VMEM((tokens, 2 * kv_cols), jnp.bfloat16),
             pltpu.VMEM((hops, tokens, 2 * kv_cols), jnp.bfloat16),
@@ -406,14 +487,15 @@
             pltpu.VMEM((back, 8, tokens), jnp.int32),
             pltpu.VMEM((heads, tokens, HD), jnp.float32),
             pltpu.VMEM((heads, tokens, 128), jnp.float32),
-            pltpu.VMEM((chunks, PAGE, 2 * kv_cols), jnp.bfloat16),
-            pltpu.VMEM((chunks, PAGE, 2 * kv_cols), jnp.bfloat16),
+            pltpu.VMEM((pages, PAGE, 2 * kv_cols), jnp.bfloat16),
+            pltpu.VMEM((pages, PAGE, 2 * kv_cols), jnp.bfloat16),
             dma((4,)),
             dma((3, chunks)), dma((3, chunks)),
             dma((hops, chunks)), dma((hops, chunks)),
             dma((hops + 1, chunks)), dma((hops + 1, chunks)),
             dma((back,)), dma((back,)),
             dma((4,)), dma((4,)),
+            dma((4,)), dma((4,)), dma((chunks,)),
         ],
         compiler_params=pltpu.CompilerParams(
             collective_id=0, has_side_effects=True, vmem_limit_bytes=56 * 1024 * 1024
@@ -427,7 +509,7 @@
     )(
         hidden, norm_gain, w_query, w_key, w_value, segment_ids, freqs, page_table
     )
-    kv_cache = cache.reshape(1, PAGE, 2, chunks * kv_cols)
+    kv_cache = cache.reshape(1, PAGE, 2, pages * kv_cols)
     return (attended, kv_cache)
 
 

time: 78.2 us -> 83.4 us (1.066); the launches traced: 77 us -> 83.2 us
  Pallas kernels: 72.5 us -> 78.7 us
    pallas_call x1, Pallas kernels: 72.5 us -> 78.7 us  [per_device(): pl.pallas_call(functools.partial(layer_kernel, n, back, hops, pages, chun...]
where the time goes in v3:
time: 83.4 us; the launch traced here: 83.2 us
  Pallas kernels  78.7 us (94%)
  local copies, waits for them, and re-layouts  3.9 us (5%)
    pallas_call x1, Pallas kernels, per_device(): pl.pallas_call(functools.partial(layer_kernel, n, back, hops, pages, chun...  78.7 us
    reshape x1, local copies, waits for them, and re-layouts, per_device(): kv_cache = cache.reshape(1, PAGE, 2, pages * kv_cols)  2.03 us
    unnamed x1, local copies, waits for them, and re-layouts  1.87 us

profile of v3, /device:TPU:27, one launch (start us, length us, event | category | flops | bytes accessed | tf_op | source)
XLA Modules:
  0.0 83.2 jit_solution(17025394562950062120)
XLA Ops:
  0.6 78.7 %shard_map.95 = (bf16[512,512]{1,0:T(8,128)(2,1)}, bf16[256,1024]{1,0:T(8,128)(2,1)}) custom-call(bf16[512,1152]{1,0:T(8,128)(2,1)} %hidden.1, f32[4608]{0:T(1024)} %gain_flat.1, bf16[4608,512]{1,0:T(8,128)(2,1)} %w_query.1, bf16[4608,256]{1,0:T(8,128)(2,1)} %w_key.1, bf16[4608,256]{1,0:T(8,128)(2,1)} %w_value.1, s32[512]{0:T(512)} %ids_flat.1, ...), custom_call_target="tpu_custom_call" | custom-call | flops 9126805504 | bytes 9437184 | tf_op jit(solution)/shard_map/pallas_call | solution.py:457
  79.3 2.0 %reshape.7 = bf16[1,128,2,1024]{3,2,1,0:T(2,128)(2,1)} reshape(bf16[256,1024]{1,0:T(8,128)(2,1)} %get-tuple-element.5) | data formatting | bytes 1048576 | tf_op jit(solution)/shard_map/reshape | solution.py:512
  81.3 1.9 %copy.11 = bf16[512,512]{1,0:T(8,128)(2,1)} copy(bf16[512,512]{1,0:T(8,128)(2,1)} %get-tuple-element.8) | data formatting | bytes 1048576
